TPU v7x, 256 devices: a whole 4x4x8 slice. The times are simulated.
256 devices in a mesh: occ: 16 (over z_lo, x), aux: 16 (over y, z_hi, core).
Axes of the slice: x: 4, y: 4, z: 8 (z_hi: 2, z_lo: 4; z = z_hi * 4 + z_lo), core: 2. Of those that a mesh axis runs over, the one named last changes fastest.
Arguments:
- factor: bfloat16 [16, 96, 256, 256], P('occ', 'aux'), may hold values from -0.375 to 0.375
- amplitudes: bfloat16 [512, 256, 256], P('occ'), may hold values from -0.625 to 0.625
- pair_domain: int32 [512], P('occ'), may hold values from 0 to 15, as said below
- pair_count: int32 [16], replicated, may hold values from 1 to 32, 256 in all
Outputs:
- ladder: float32 [512, 256, 256], P('occ', 'aux')
Inputs may be any that keep to these rules, and one draw needn't show every extreme that they name: `pair_domain`: among the 32 slots of one occupied block at most 3 name one domain block, and some domain block is named by exactly 3 of them in every occupied block. `pair_count`: the largest count equals 32 in every draw.
All inputs are finite; a program needn't handle non-finite values.
Results may differ from a plain program's by a relative error of at most 0.0029.
Values may be sent and summed in bfloat16 or wider, within the bound.
A program may use at most 128 MiB of HBM per device.

v0:
```python
import jax
import jax.numpy as jnp
from jax import lax
from jax.sharding import PartitionSpec as P


def per_device(factor, amplitudes, pair_domain, pair_count):
    slots = amplitudes.shape[0]
    block_width = amplitudes.shape[1]
    mine_index = lax.axis_index("occ")
    own_count = lax.dynamic_index_in_dim(pair_count, mine_index, 0, keepdims=False)
    live = jnp.arange(slots, dtype=jnp.int32) < own_count
    initial = jnp.zeros((slots, block_width, block_width), jnp.float32)
    piece = lax.all_gather(factor, "occ", axis=0, tiled=True)
    start = jnp.int32(0)
    blocks_here = piece.shape[0]

    def visit(slot, carry):
        domain = pair_domain[slot]
        take = live[slot] & (domain >= start) & (domain < start + blocks_here)

        def compute(inner):
            local_index = jnp.clip(domain, 0, blocks_here - 1)
            block = lax.dynamic_index_in_dim(piece, local_index, 0, keepdims=False)
            amp = lax.dynamic_index_in_dim(amplitudes, slot, 0, keepdims=False)
            half = jnp.einsum("qac,cd->qad", block, amp, preferred_element_type=jnp.float32).astype(
                jnp.bfloat16
            )
            term = jnp.einsum("qad,qbd->ab", half, block, preferred_element_type=jnp.float32)
            return inner.at[slot].add(term)

        def keep_same(inner):
            return inner

        return lax.cond(take, compute, keep_same, carry)

    partial_sum = lax.fori_loop(0, slots, visit, initial)
    return lax.psum_scatter(partial_sum, "aux", scatter_dimension=1, tiled=True)


def solution(mesh):
    placed = (P("occ", "aux", None, None), P("occ", None, None), P("occ"), P())
    return jax.shard_map(
        per_device, mesh=mesh, in_specs=placed, out_specs=P("occ", "aux", None), check_vma=False
    )
```

profile of v0, /device:TPU:1, one launch (start us, length us, event | category | flops | bytes accessed | tf_op | source)
XLA Modules:
  0.0 577.6 jit_solution(1003618527904770154)
XLA Ops:
  9.2 148.4 %all-gather.2.cloned.1.call-done = bf16[16,6,256,256]{3,2,1,0:T(8,128)(2,1)} async-done(((bf16[1,6,256,256]{3,2,1,0:T(8,128)(2,1)}), bf16[16,6,256,256]{3,2,1,0:T(8,128)(2,1)}) %all-gather.2.cloned.1.call-update) | async-done | bytes 12582928 | tf_op jit(solution)/shard_map/all_gather | solution.py:14
  157.6 4.2 broadcast_in_dim.4
  161.7 269.9 %while.17 = (s32[]{:T(128)}, f32[32,256,256]{2,1,0:T(8,128)}, pred[32]{0:T(512)(128)(4,1)S(1)}, s32[32]{0:T(128)S(1)}, bf16[16,6,256,256]{3,2,1,0:T(8,128)(2,1)}...) while((s32[]{:T(128)}, f32[32,256,256]{2,1,0:T(8,128)}, ...), condition=%wide.region_4.5_spmd, body=%wide.region_0.4_spmd.sunk | while | flops 403177504 | bytes 2231051 | solution.py:37
  164.7 5.5 conditional.2
  166.7 3.5 fusion.4
  173.1 5.5 conditional.2
  175.1 3.6 fusion.4
  181.6 5.5 conditional.2
  190.0 5.5 conditional.2
  198.5 5.5 conditional.2
  206.9 5.5 conditional.2
  215.3 5.5 conditional.2
  223.7 5.5 conditional.2
  225.6 3.6 fusion.4
  232.2 5.6 conditional.2
  234.1 3.6 fusion.4
  240.7 5.5 conditional.2
  249.1 5.5 conditional.2
  257.5 5.5 conditional.2
  259.5 3.5 fusion.4
  265.9 5.5 conditional.2
  267.9 3.6 fusion.4
  274.4 5.5 conditional.2
  282.8 5.5 conditional.2
  291.2 5.5 conditional.2
  299.6 5.5 conditional.2
  308.0 5.5 conditional.2
  310.0 3.5 fusion.4
  316.5 5.5 conditional.2
  318.5 3.5 fusion.4
  324.9 5.5 conditional.2
  333.3 5.5 conditional.2
  335.3 3.5 fusion.4
  341.8 5.5 conditional.2
  350.2 5.5 conditional.2
  358.6 5.5 conditional.2
  360.6 3.6 fusion.4
  367.1 5.5 conditional.2
  375.5 5.5 conditional.2
  383.9 5.5 conditional.2
  392.3 5.6 conditional.2
  394.3 3.6 fusion.4
  400.8 5.5 conditional.2
  409.2 5.5 conditional.2
  417.7 5.5 conditional.2
  419.6 3.6 fusion.4
  426.1 5.5 conditional.2
  431.6 139.1 %reduce-scatter.2.cloned.1.call-done = f32[32,16,256]{2,1,0:T(8,128)} async-done(((f32[32,256,256]{2,1,0:T(8,128)}), f32[32,16,256]{2,1,0:T(8,128)}) %reduce-scatter.2.cloned.1.call-update) | async-done | bytes 524304 | tf_op jit(solution)/shard_map/reduce_scatter | solution.py:38
  (124 shorter events, 153.8 us)
Async XLA Ops:
  6.5 155.2 %copy-start = (s32[32]{0:T(128)S(1)}, s32[32]{0:T(128)}, u32[]{:S(2)}) copy-start(s32[32]{0:T(128)} %param.12) | copy-start | bytes 388
  6.5 151.0 %all-gather.2.cloned.1.call-start = ((), (), s32[]{:S(2)}) async-start(), calls=%async_computation.1 | async-start | bytes 13369344 | tf_op jit(solution)/shard_map/all_gather | solution.py:14
  7.3 563.5 %reduce-scatter.2.cloned.1.call-start = ((), (), s32[]{:S(2)}) async-start(), calls=%async_computation.2 | async-start | bytes 8912896 | tf_op jit(solution)/shard_map/reduce_scatter | solution.py:38
Sparse Core Ops, SparseCore 0:
  9.1 148.3 all-gather.1
  431.8 138.9 reduce-scatter.1
where the time goes:
time: 580 us; the launch traced here: 578 us
  waiting for transfers between devices  288 us (50%)
  matrix products  113 us (19%)
  loops' own time  76.1 us (13%)
  other arithmetic  44.8 us (8%)
  local copies, waits for them, and re-layouts  42.5 us (7%)
  between operations  13.4 us (2%)
    all_gather x1, waiting for transfers between devices, per_device(): piece = lax.all_gather(factor, 'occ', axis=0, tiled=True)  148 us
    reduce_scatter x1, waiting for transfers between devices, per_device(): return lax.psum_scatter(partial_sum, 'aux', scatter_dimension=1, tiled=True)  139 us
    dot_general x32, matrix products, compute(): jnp.einsum('qad,qbd->ab', half, block, preferred_element_type=jnp.float32)  113 us
    another operation x1, loops' own time, per_device(): partial_sum = lax.fori_loop(0, slots, visit, initial)  56.9 us
    another operation x32, other arithmetic  44.1 us
    dynamic_slice x32, local copies, waits for them, and re-layouts, visit(): take = live[slot] & (domain >= start) & (domain < start + blocks_here)  19.3 us
    another operation x32, loops' own time, visit(): return lax.cond(take, compute, keep_same, carry)  19.1 us
    dynamic_slice x32, local copies, waits for them, and re-layouts, visit(): domain = pair_domain[slot]  17.8 us
  transfers between devices with their start and end apart: 2, of which 2 were waited for; matrix products, arithmetic and copies ran while one was open for 0% of the time, Pallas kernels for 0%

commit v1 on v0

v1 whole, which is shorter than its diff:
```python
import jax
import jax.numpy as jnp
from jax import lax
from jax.experimental import pallas as pl
from jax.experimental.pallas import tpu as pltpu
from jax.sharding import PartitionSpec as P

MESH = pl.DeviceIdType.MESH
NT = (((1,), (1,)), ((), ()))
NQ = 3
CHUNKS = 16
CAP = 3
ROWS = 16


def kernel(
    factor, amps, domain, count, out,
    fbuf, ampv, packed, arecv, acc, ebuf, erecv, rank,
    fsend, frecv, asend, arecv_sem, esend, erecv_sem, local_sem,
):
    me_o, me_a = lax.axis_index("occ"), lax.axis_index("aux")
    z, x = me_o // 4, me_o % 4
    y, zh, core = me_a // 4, (me_a // 2) % 2, me_a % 2
    up = ((y + 1) % 4) * 4 + me_a % 4
    down = ((y + 3) % 4) * 4 + me_a % 4
    sibling = me_a + 1 - 2 * core

    def shift(j):
        dx = core + 2 * j
        return dx, (dx + y) % 4

    def ahead(j):
        dx, dz = shift(j)
        return ((z + dz) % 4) * 4 + (x + dx) % 4

    def behind(j):
        dx, dz = shift(j)
        return ((z + 4 - dz) % 4) * 4 + (x + 4 - dx) % 4

    def server(i):
        dx, dz, half = i % 4, (i // 4) % 4, i // 16
        src_o = ((z + dz) % 4) * 4 + (x + dx) % 4
        src_a = (((dz + 4 - dx) % 4) * 2 + half) * 2 + dx % 2
        return src_o, src_a, half

    get_factor = pltpu.make_async_copy(factor, fbuf.at[pl.ds(0, 2)], local_sem.at[0])
    get_amps = pltpu.make_async_copy(amps, ampv, local_sem.at[1])
    get_factor.start()
    get_amps.start()

    barrier = pltpu.get_barrier_semaphore()
    for peer in (up, down, sibling):
        pl.semaphore_signal(barrier, inc=1, device_id=(me_o, peer), device_id_type=MESH)
    for j in range(2):
        src = behind(j)

        @pl.when(src != me_o)
        def _():
            pl.semaphore_signal(barrier, inc=1, device_id=(src, me_a), device_id_type=MESH)

    def greet(i, carry):
        src_o, src_a, _ = server(i)

        @pl.when(jnp.logical_or(src_o != me_o, src_a != me_a))
        def _():
            pl.semaphore_signal(barrier, inc=1, device_id=(src_o, src_a), device_id_type=MESH)

        return carry

    lax.fori_loop(0, 32, greet, 0)
    at_home = jnp.where(jnp.logical_and(y == 0, core == 0), 1, 0)

    def find(p, carry):
        own = domain[p]

        def earlier(q, k):
            return k + jnp.where(domain[q] == own, 1, 0)

        rank[p] = lax.fori_loop(0, p, earlier, 0)
        new = []
        for j in range(2):
            seen, picks = carry[j]
            hit = own == ahead(j)
            picks = tuple(jnp.where(jnp.logical_and(hit, seen == k), p, picks[k]) for k in range(CAP))
            new.append((seen + jnp.where(hit, 1, 0), picks))
        return tuple(new)

    zero = jnp.int32(0)
    start = (zero, (zero, zero, zero))
    found = lax.fori_loop(0, 32, find, (start, start))

    pl.semaphore_wait(barrier, 37 - 2 * at_home)

    def fcopy(src, dst, n, peer):
        return pltpu.make_async_remote_copy(
            src_ref=fbuf.at[src], dst_ref=fbuf.at[dst], send_sem=fsend.at[n], recv_sem=frecv.at[dst],
            device_id=(me_o, peer), device_id_type=MESH,
        )

    get_factor.wait()
    sends = [
        fcopy(0, 4, 0, up), fcopy(1, 5, 1, down), fcopy(0, 2, 2, sibling), fcopy(1, 3, 3, sibling),
        fcopy(1, 8, 4, up), fcopy(0, 9, 5, down),
    ]
    for c in sends:
        c.start()
    later = {
        4: [fcopy(4, 12, 6, up), fcopy(4, 6, 7, sibling)],
        5: [fcopy(5, 13, 8, down), fcopy(5, 7, 9, sibling)],
        8: [fcopy(8, 10, 10, sibling)],
        9: [fcopy(9, 11, 11, sibling)],
        12: [fcopy(12, 14, 12, sibling)],
        13: [fcopy(13, 15, 13, sibling)],
    }
    recvd = {dst: fcopy(dst, dst, 0, sibling) for dst in range(2, CHUNKS)}

    def arrive(*chunks):
        for c in chunks:
            recvd[c].wait_recv()
            for more in later.get(c, ()):
                more.start()

    get_amps.wait()

    def acopy(j, k, dst_o):
        s = j * CAP + k
        return pltpu.make_async_remote_copy(
            src_ref=packed.at[s], dst_ref=arecv.at[s], send_sem=asend.at[s], recv_sem=arecv_sem.at[s],
            device_id=(dst_o, me_a), device_id_type=MESH,
        )

    for k in range(CAP):
        for j in range(2):
            s = j * CAP + k
            packed[s] = ampv[found[j][1][k]]
            dst = ahead(j)

            @pl.when(dst != me_o)
            def _():
                acopy(j, k, dst).start()

            @pl.when(dst == me_o)
            def _():
                pltpu.make_async_copy(packed.at[s], arecv.at[s], arecv_sem.at[s]).start()

    def amps_arrive(k):
        for j in range(2):
            acopy(j, k, me_o).wait_recv()

    acc[...] = jnp.zeros(acc.shape, jnp.float32)

    def compute(chunk, slots):
        b = fbuf[chunk]
        tall = b.reshape(NQ * 256, 256)
        wide = jnp.concatenate([b[q] for q in range(NQ)], axis=1)
        for s in slots:
            half = jnp.dot(tall, arecv[s], preferred_element_type=jnp.float32).astype(jnp.bfloat16)
            half = jnp.concatenate([half[q * 256:(q + 1) * 256] for q in range(NQ)], axis=1)
            acc[s] += lax.dot_general(half, wide, NT, preferred_element_type=jnp.float32)

    def compute_run(first, stop, slots):
        def body(i, carry):
            compute(i, slots)
            return carry

        lax.fori_loop(first, stop, body, 0)

    k0, k1, k2 = (0, 3), (1, 4), (2, 5)
    every = (0, 3, 1, 4, 2, 5)
    amps_arrive(0)
    arrive(2, 3)
    compute_run(0, 4, k0)
    arrive(4, 5)
    compute_run(4, 6, k0)
    amps_arrive(1)
    compute_run(0, 6, k1)
    arrive(6, 7)
    compute_run(6, 8, k0 + k1)
    arrive(8, 9)
    compute_run(8, 10, k0 + k1)
    amps_arrive(2)
    compute_run(0, 10, k2)
    arrive(10, 11)
    compute_run(10, 12, every)
    arrive(12, 13)
    compute_run(12, 14, every)
    arrive(14, 15)

    def ecopy(j, a, dst_o):
        n = j * 16 + a
        return pltpu.make_async_remote_copy(
            src_ref=ebuf.at[j, :, pl.ds(pl.multiple_of(a * ROWS, ROWS), ROWS), :],
            dst_ref=erecv.at[zh * 16 + me_o],
            send_sem=esend.at[n], recv_sem=erecv_sem.at[zh * 16 + me_o],
            device_id=(dst_o, a), device_id_type=MESH,
        )

    for j in range(2):
        compute_run(14, 16, tuple(range(j * CAP, (j + 1) * CAP)))
        for k in range(CAP):
            ebuf[j, k] = acc[j * CAP + k].astype(jnp.bfloat16)
        dst_o = behind(j)

        def give(a, carry):
            away = jnp.logical_or(dst_o != me_o, a != me_a)

            @pl.when(away)
            def _():
                ecopy(j, a, dst_o).start()

            @pl.when(jnp.logical_not(away))
            def _():
                pltpu.make_async_copy(
                    ebuf.at[j, :, pl.ds(pl.multiple_of(a * ROWS, ROWS), ROWS), :],
                    erecv.at[zh * 16 + me_o], erecv_sem.at[zh * 16 + me_o],
                ).start()

            return carry

        lax.fori_loop(0, 16, give, 0)

    def take(i, carry):
        pltpu.make_async_copy(erecv.at[i], erecv.at[i], erecv_sem.at[i]).wait()
        return carry

    lax.fori_loop(0, 32, take, 0)

    live = count[me_o]

    def unpack(p, carry):
        d, k = jnp.clip(domain[p], 0, 15), jnp.minimum(rank[p], CAP - 1)
        term = erecv[d, k].astype(jnp.float32) + erecv[16 + d, k].astype(jnp.float32)
        out[p] = jnp.where(p < live, term, 0.0)
        return carry

    lax.fori_loop(0, 32, unpack, 0)

    for c in sends:
        c.wait_send()
    for group in later.values():
        for c in group:
            c.wait_send()
    for j in range(2):
        dst = ahead(j)

        @pl.when(dst != me_o)
        def _():
            for k in range(CAP):
                acopy(j, k, dst).wait_send()

        dst_o = behind(j)

        def sent(a, carry):
            @pl.when(jnp.logical_or(dst_o != me_o, a != me_a))
            def _():
                ecopy(j, a, dst_o).wait_send()

            return carry

        lax.fori_loop(0, 16, sent, 0)


def per_device(factor, amplitudes, pair_domain, pair_count):
    hbm = pl.BlockSpec(memory_space=pl.ANY)
    smem = pl.BlockSpec(memory_space=pltpu.SMEM)
    wide = (256, 256)
    return pl.pallas_call(
        kernel,
        out_shape=jax.ShapeDtypeStruct((32, ROWS, 256), jnp.float32),
        in_specs=[hbm, hbm, smem, smem],
        out_specs=pl.BlockSpec(memory_space=pltpu.VMEM),
        scratch_shapes=[
            pltpu.VMEM((CHUNKS, NQ) + wide, jnp.bfloat16),
            pltpu.VMEM((32,) + wide, jnp.bfloat16),
            pltpu.VMEM((2 * CAP,) + wide, jnp.bfloat16),
            pltpu.VMEM((2 * CAP,) + wide, jnp.bfloat16),
            pltpu.VMEM((2 * CAP,) + wide, jnp.float32),
            pltpu.VMEM((2, CAP) + wide, jnp.bfloat16),
            pltpu.VMEM((32, CAP, ROWS, 256), jnp.bfloat16),
            pltpu.SMEM((32,), jnp.int32),
            pltpu.SemaphoreType.DMA((14,)),
            pltpu.SemaphoreType.DMA((CHUNKS,)),
            pltpu.SemaphoreType.DMA((2 * CAP,)),
            pltpu.SemaphoreType.DMA((2 * CAP,)),
            pltpu.SemaphoreType.DMA((32,)),
            pltpu.SemaphoreType.DMA((32,)),
            pltpu.SemaphoreType.DMA((2,)),
        ],
        compiler_params=pltpu.CompilerParams(
            collective_id=0, has_side_effects=True, vmem_limit_bytes=48 * 2**20
        ),
        cost_estimate=pl.CostEstimate(flops=20 * 10**9, bytes_accessed=6 * 10**6, transcendentals=0),
    )(factor.reshape(2, NQ, 256, 256), amplitudes, pair_domain, pair_count)


def solution(mesh):
    placed = (P("occ", "aux", None, None), P("occ", None, None), P("occ"), P())
    return jax.shard_map(
        per_device, mesh=mesh, in_specs=placed, out_specs=P("occ", "aux", None), check_vma=False
    )
```

time: 580 us -> 82.1 us (0.14)
  waiting for transfers between devices: 288 us -> 0 us
  matrix products: 113 us -> 0 us
  Pallas kernels: 0 us -> 76.5 us
  loops' own time: 76.1 us -> 0 us
  other arithmetic: 44.8 us -> 0 us
  local copies, waits for them, and re-layouts: 42.5 us -> 5.43 us
  between operations: 13.4 us -> 0.01 us
    all_gather x1 -> x0, waiting for transfers between devices: 148 us -> none  [per_device(): piece = lax.all_gather(factor, 'occ', axis=0, tiled=True)]
    reduce_scatter x1 -> x0, waiting for transfers between devices: 139 us -> none  [per_device(): return lax.psum_scatter(partial_sum, 'aux', scatter_dimension=1, tiled=True)]
    dot_general x32 -> x0, matrix products: 113 us -> none  [compute(): jnp.einsum('qad,qbd->ab', half, block, preferred_element_type=jnp.float32)]
    pallas_call x0 -> x1, Pallas kernels: none -> 76.5 us  [per_device(): pl.pallas_call(kernel, out_shape=jax.ShapeDtypeStruct((32, ROWS, 256), jn...]
    another operation x33 -> x0, loops' own time: 76.1 us -> none  [the longest x1 56.9 us: per_device(): partial_sum = lax.fori_loop(0, slots, visit, initial)]
    another operation x32 -> x0, other arithmetic: 44.1 us -> none
    dynamic_slice x65 -> x0, local copies, waits for them, and re-layouts: 38.3 us -> none  [the longest x32 19.3 us: visit(): take = live[slot] & (domain >= start) & (domain < start + blocks_here)]
  transfers between devices with their start and end apart: 2 -> 0, of which waited for: 2 -> 0; matrix products, arithmetic and copies ran while one was open for 0% -> 0% of each run, Pallas kernels for 0% -> 0%
where the time goes in v1:
time: 82.1 us; the launch traced here: 81.9 us
  Pallas kernels  76.5 us (93%)
  local copies, waits for them, and re-layouts  5.43 us (7%)
    pallas_call x1, Pallas kernels, per_device(): pl.pallas_call(kernel, out_shape=jax.ShapeDtypeStruct((32, ROWS, 256), jn...  76.5 us
    unnamed x9, local copies, waits for them, and re-layouts  5.43 us

profile of v1, /device:TPU:1, one launch (start us, length us, event | category | flops | bytes accessed | tf_op | source)
XLA Modules:
  0.0 81.9 jit_solution(7295732962849207341)
XLA Ops:
  0.0 0.0 copy-start
  0.0 2.2 %copy-done = bf16[32,256,256]{2,1,0:T(8,128)(2,1)S(1)} copy-done((bf16[32,256,256]{2,1,0:T(8,128)(2,1)S(1)}, bf16[32,256,256]{2,1,0:T(8,128)(2,1)}, u32[]{:S(2)}) %copy-start) | copy-done | bytes 4194328
  2.2 0.0 copy-start.1
  2.2 1.1 %copy-done.1 = bf16[1,6,256,256]{3,2,1,0:T(8,128)(2,1)S(1)} copy-done((bf16[1,6,256,256]{3,2,1,0:T(8,128)(2,1)S(1)}, bf16[1,6,256,256]{3,2,1,0:T(8,128)(2,1)}, u32[]{:S(2)}) %copy-start.1) | copy-done | bytes 786456
  3.3 0.0 copy-start.2
  3.3 0.7 copy-done.2
  4.0 0.0 copy-start.3
  4.0 0.7 copy-done.3
  4.6 76.5 %shard_map.46 = f32[32,16,256]{2,1,0:T(8,128)S(1)} custom-call(bf16[2,3,256,256]{3,2,1,0:T(8,128)(2,1)S(1)} %bitcast.1, bf16[32,256,256]{2,1,0:T(8,128)(2,1)S(1)} %copy-done, s32[32]{0:T(128)S(1)} %copy-done.2, s32[16]{0:T(128)S(1)} %copy-done.3), custom_call_target="tpu_custom_call" | custom-call | flops 20000000000 | bytes 6000000 | tf_op jit(solution)/shard_map/pallas_call | solution.py:267
  81.1 0.8 copy.6
Async XLA Ops:
  0.0 2.2 %copy-start = (bf16[32,256,256]{2,1,0:T(8,128)(2,1)S(1)}, bf16[32,256,256]{2,1,0:T(8,128)(2,1)}, u32[]{:S(2)}) copy-start(bf16[32,256,256]{2,1,0:T(8,128)(2,1)} %amps.1) | copy-start | bytes 12582916
  2.2 1.1 %copy-start.1 = (bf16[1,6,256,256]{3,2,1,0:T(8,128)(2,1)S(1)}, bf16[1,6,256,256]{3,2,1,0:T(8,128)(2,1)}, u32[]{:S(2)}) copy-start(bf16[1,6,256,256]{3,2,1,0:T(8,128)(2,1)} %param.4) | copy-start | bytes 2359300
  3.3 0.7 copy-start.2
  4.0 0.7 copy-start.3

commit v2 on v0

v2 whole, which is shorter than its diff:
```python
import jax
import jax.numpy as jnp
from jax import lax
from jax.experimental import pallas as pl
from jax.experimental.pallas import tpu as pltpu
from jax.sharding import PartitionSpec as P

MESH = pl.DeviceIdType.MESH
NT = (((1,), (1,)), ((), ()))
CAP = 3
SLOTS = 2 * CAP
ROWS = 16


def kernel(
    factor, amps, domain_hbm, count_hbm, out,
    fbuf, ampv, packed, arecv, acc, ebuf, erecv, domain, count, rank,
    fsend, frecv, asend, arecv_sem, esend, erecv_sem, local_sem, ready,
):
    me_o, me_a = lax.axis_index("occ"), lax.axis_index("aux")
    z, x = me_o // 4, me_o % 4
    y, zh, core = me_a // 4, (me_a // 2) % 2, me_a % 2
    up = ((y + 1) % 4) * 4 + me_a % 4
    down = ((y + 3) % 4) * 4 + me_a % 4
    sibling = me_a + 1 - 2 * core
    partner = me_a + 2 - 4 * zh
    z8 = zh * 4 + z

    def steps(j):
        dx = core + 2 * j
        dz = (dx + y) % 4
        return dx, dz, jnp.where(dz == 3, 7, dz)

    def ahead(j):
        dx, _, ring = steps(j)
        to = (z8 + ring) % 8
        return (to % 4) * 4 + (x + dx) % 4, (y * 2 + to // 4) * 2 + core

    def behind(j):
        dx, _, ring = steps(j)
        to = (z8 + 8 - ring) % 8
        return (to % 4) * 4 + (x + 4 - dx) % 4, (y * 2 + to // 4) * 2 + core

    get_factor = pltpu.make_async_copy(factor, fbuf.at[pl.ds(0, 6)], local_sem.at[0])
    get_amps = pltpu.make_async_copy(amps, ampv, local_sem.at[1])
    get_domain = pltpu.make_async_copy(domain_hbm, domain, local_sem.at[2])
    get_count = pltpu.make_async_copy(count_hbm, count, local_sem.at[3])
    get_domain.start()
    get_factor.start()
    get_amps.start()
    get_count.start()

    barrier = pltpu.get_barrier_semaphore()
    for peer in (up, down, sibling, partner):
        pl.semaphore_signal(barrier, inc=1, device_id=(me_o, peer), device_id_type=MESH)
    targets = [ahead(j) for j in range(2)]
    origins = [behind(j) for j in range(2)]
    for j in range(2):
        src = origins[j]

        @pl.when(src[0] != me_o)
        def _():
            pl.semaphore_signal(barrier, inc=1, device_id=src, device_id_type=MESH)

    def find(p, carry):
        own = domain[p]
        new = []
        for j in range(2):
            seen, picks = carry[j]
            hit = own == targets[j][0]
            picks = tuple(jnp.where(jnp.logical_and(hit, seen == k), p, picks[k]) for k in range(CAP))
            new.append((seen + jnp.where(hit, 1, 0), picks))
        return tuple(new)

    get_domain.wait()
    zero = jnp.int32(0)
    start = (zero, (zero, zero, zero))
    found = lax.fori_loop(0, 32, find, (start, start))

    at_home = jnp.where(jnp.logical_and(y == 0, core == 0), 1, 0)
    pl.semaphore_wait(barrier, 6 - at_home)

    def fcopy(src, dst, size, n, peer):
        return pltpu.make_async_remote_copy(
            src_ref=fbuf.at[pl.ds(src, size)], dst_ref=fbuf.at[pl.ds(dst, size)],
            send_sem=fsend, recv_sem=frecv.at[n], device_id=(me_o, peer), device_id_type=MESH,
        )

    def arrived(first, size, n):
        ref = fbuf.at[pl.ds(first, size)]
        pltpu.make_async_copy(ref, ref, frecv.at[n]).wait()

    get_factor.wait()
    fcopy(0, 12, 3, 0, up).start()
    fcopy(3, 15, 3, 0, down).start()
    fcopy(0, 6, 6, 1, sibling).start()
    get_amps.wait()

    def amps_go(k):
        for j in range(2):
            src, dst = packed.at[j, k], arecv.at[2 * k + j]
            packed[j, k] = ampv[found[j][1][k]]

            @pl.when(targets[j][0] != me_o)
            def _():
                pltpu.make_async_remote_copy(
                    src_ref=src, dst_ref=dst, send_sem=asend.at[j], recv_sem=arecv_sem.at[k],
                    device_id=targets[j], device_id_type=MESH,
                ).start()

            @pl.when(targets[j][0] == me_o)
            def _():
                pltpu.make_async_copy(src, dst, arecv_sem.at[k]).start()

    def amps_arrive(k):
        ref = arecv.at[pl.ds(2 * k, 2)]
        pltpu.make_async_copy(ref, ref, arecv_sem.at[k]).wait()

    for k in range(CAP):
        amps_go(k)
    fcopy(3, 24, 3, 2, up).start()
    fcopy(0, 27, 3, 2, down).start()

    def tell(n, device):
        pl.semaphore_signal(ready.at[n], inc=1, device_id=device, device_id_type=MESH)

    def hear(n):
        pl.semaphore_wait(ready.at[n], 1)

    tell(0, (me_o, sibling))

    def place(p, carry):
        own = domain[p]
        before = zero
        for q in range(31):
            before += jnp.where(jnp.logical_and(domain[q] == own, q < p), 1, 0)
        rank[p] = before
        return carry

    lax.fori_loop(0, 32, place, 0)
    get_count.wait()
    acc[...] = jnp.zeros(acc.shape, jnp.float32)

    def compute(first, size, slots):
        b = fbuf[pl.ds(first, size)]
        tall = b.reshape(size * 256, 256)
        wide = jnp.concatenate([b[q] for q in range(size)], axis=1)
        for s in slots:
            half = jnp.dot(tall, arecv[s], preferred_element_type=jnp.float32).astype(jnp.bfloat16)
            half = jnp.concatenate([half[q * 256:(q + 1) * 256] for q in range(size)], axis=1)
            acc[s] += lax.dot_general(half, wide, NT, preferred_element_type=jnp.float32)

    hear(0)
    tell(1, (me_o, partner))

    def places(first, stop, k):
        def body(i, carry):
            compute(6 * i, 6, (2 * k, 2 * k + 1))
            return carry

        lax.fori_loop(first, stop, body, 0)

    def ranks(place):
        def body(k, carry):
            compute(6 * place, 6, (2 * k, 2 * k + 1))
            return carry

        lax.fori_loop(0, 2, body, 0)

    arrived(6, 6, 1)
    amps_arrive(0)
    places(0, 2, 0)
    amps_arrive(1)
    places(0, 2, 1)
    arrived(12, 6, 0)
    for g in range(3):
        fcopy(12 + g, 36 + 4 * g, 1, 3 + g, up).start()
        fcopy(15 + g, 37 + 4 * g, 1, 3 + g, down).start()
    fcopy(12, 18, 6, 6, sibling).start()
    hear(1)
    tell(2, (me_o, up))
    tell(3, (me_o, down))
    ranks(2)
    arrived(18, 6, 6)
    ranks(3)
    amps_arrive(2)
    hear(2)
    hear(3)
    tell(4, (me_o, up))
    places(0, 4, 2)
    hear(4)
    for j in range(2):
        @pl.when(targets[j][0] != me_o)
        def _():
            tell(5 + j, targets[j])

    def relay(g):
        arrived(36 + 4 * g, 2, 3 + g)
        fcopy(36 + 4 * g, 38 + 4 * g, 2, 8 + g, sibling).start()

    arrived(24, 6, 2)
    fcopy(24, 30, 6, 7, sibling).start()
    compute(24, 6, range(SLOTS))
    relay(0)
    arrived(30, 6, 7)
    compute(30, 6, range(SLOTS))
    for g in range(2):
        relay(g + 1)
        arrived(38 + 4 * g, 2, 8 + g)
        compute(36 + 4 * g, 4, range(SLOTS))
    for j in range(2):
        @pl.when(origins[j][0] != me_o)
        def _():
            hear(5 + j)
    arrived(46, 2, 10)

    place_here = zh * 16 + me_o
    for j in range(2):
        compute(44, 4, range(j, SLOTS, 2))
        for k in range(CAP):
            ebuf[j, k] = acc[2 * k + j].astype(jnp.bfloat16)
        home = origins[j][0] == me_o

        def give(i, carry):
            a = (me_a + i) % 16
            src = ebuf.at[j, :, pl.ds(pl.multiple_of(a * ROWS, ROWS), ROWS), :]
            here = jnp.logical_and(home, i == 0)

            @pl.when(jnp.logical_not(here))
            def _():
                pltpu.make_async_remote_copy(
                    src_ref=src, dst_ref=erecv.at[place_here], send_sem=esend.at[j], recv_sem=erecv_sem,
                    device_id=(origins[j][0], a), device_id_type=MESH,
                ).start()

            @pl.when(here)
            def _():
                pltpu.make_async_copy(src, erecv.at[place_here], erecv_sem).start()

            return carry

        lax.fori_loop(0, 16, give, 0)

    def sent(ref, sem):
        pltpu.make_async_copy(ref, ref, sem).wait()

    sent(fbuf.at[pl.ds(0, 42)], fsend)
    for j in range(2):
        @pl.when(targets[j][0] != me_o)
        def _():
            sent(packed.at[j], asend.at[j])

    pltpu.make_async_copy(erecv, erecv, erecv_sem).wait()

    live = count[me_o]

    def unpack(p, carry):
        d, k = jnp.clip(domain[p], 0, 15), jnp.minimum(rank[p], CAP - 1)
        term = erecv[d, k].astype(jnp.float32) + erecv[16 + d, k].astype(jnp.float32)
        out[p] = jnp.where(p < live, term, 0.0)
        return carry

    lax.fori_loop(0, 32, unpack, 0)

    for j in range(2):
        @pl.when(origins[j][0] != me_o)
        def _():
            sent(ebuf.at[j], esend.at[j])

        @pl.when(origins[j][0] == me_o)
        def _():
            sent(ebuf.at[j, :, pl.ds(0, 15 * ROWS), :], esend.at[j])


def per_device(factor, amplitudes, pair_domain, pair_count):
    hbm = pl.BlockSpec(memory_space=pl.ANY)
    square = (256, 256)
    return pl.pallas_call(
        kernel,
        out_shape=jax.ShapeDtypeStruct((32, ROWS, 256), jnp.float32),
        in_specs=[hbm, hbm, hbm, hbm],
        out_specs=pl.BlockSpec(memory_space=pltpu.VMEM),
        scratch_shapes=[
            pltpu.VMEM((48,) + square, jnp.bfloat16),
            pltpu.VMEM((32,) + square, jnp.bfloat16),
            pltpu.VMEM((2, CAP) + square, jnp.bfloat16),
            pltpu.VMEM((SLOTS,) + square, jnp.bfloat16),
            pltpu.VMEM((SLOTS,) + square, jnp.float32),
            pltpu.VMEM((2, CAP) + square, jnp.bfloat16),
            pltpu.VMEM((32, CAP, ROWS, 256), jnp.bfloat16),
            pltpu.SMEM((32,), jnp.int32),
            pltpu.SMEM((16,), jnp.int32),
            pltpu.SMEM((32,), jnp.int32),
            pltpu.SemaphoreType.DMA,
            pltpu.SemaphoreType.DMA((11,)),
            pltpu.SemaphoreType.DMA((2,)),
            pltpu.SemaphoreType.DMA((CAP,)),
            pltpu.SemaphoreType.DMA((2,)),
            pltpu.SemaphoreType.DMA,
            pltpu.SemaphoreType.DMA((4,)),
            pltpu.SemaphoreType.REGULAR((7,)),
        ],
        compiler_params=pltpu.CompilerParams(
            collective_id=0, has_side_effects=True, vmem_limit_bytes=64 * 2**20 - 2**16
        ),
        cost_estimate=pl.CostEstimate(flops=20 * 10**9, bytes_accessed=6 * 10**6, transcendentals=0),
    )(factor.reshape(6, 256, 256), amplitudes, pair_domain, pair_count)


def solution(mesh):
    placed = (P("occ", "aux", None, None), P("occ", None, None), P("occ"), P())
    return jax.shard_map(
        per_device, mesh=mesh, in_specs=placed, out_specs=P("occ", "aux", None), check_vma=False
    )
```

time: 580 us -> 66.9 us (0.12)
  waiting for transfers between devices: 288 us -> 0 us
  matrix products: 113 us -> 0 us
  loops' own time: 76.1 us -> 0 us
  Pallas kernels: 0 us -> 64.9 us
  other arithmetic: 44.8 us -> 0 us
  local copies, waits for them, and re-layouts: 42.5 us -> 1.87 us
  between operations: 13.4 us -> 0.01 us
    all_gather x1 -> x0, waiting for transfers between devices: 148 us -> none  [per_device(): piece = lax.all_gather(factor, 'occ', axis=0, tiled=True)]
    reduce_scatter x1 -> x0, waiting for transfers between devices: 139 us -> none  [per_device(): return lax.psum_scatter(partial_sum, 'aux', scatter_dimension=1, tiled=True)]
    dot_general x32 -> x0, matrix products: 113 us -> none  [compute(): jnp.einsum('qad,qbd->ab', half, block, preferred_element_type=jnp.float32)]
    another operation x33 -> x0, loops' own time: 76.1 us -> none  [the longest x1 56.9 us: per_device(): partial_sum = lax.fori_loop(0, slots, visit, initial)]
    pallas_call x0 -> x1, Pallas kernels: none -> 64.9 us  [per_device(): pl.pallas_call(kernel, out_shape=jax.ShapeDtypeStruct((32, ROWS, 256), jn...]
    another operation x32 -> x0, other arithmetic: 44.1 us -> none
    dynamic_slice x65 -> x0, local copies, waits for them, and re-layouts: 38.3 us -> none  [the longest x32 19.3 us: visit(): take = live[slot] & (domain >= start) & (domain < start + blocks_here)]
  transfers between devices with their start and end apart: 2 -> 0, of which waited for: 2 -> 0; matrix products, arithmetic and copies ran while one was open for 0% -> 0% of each run, Pallas kernels for 0% -> 0%
where the time goes in v2:
time: 66.9 us; the launch traced here: 66.7 us
  Pallas kernels  64.9 us (97%)
  local copies, waits for them, and re-layouts  1.87 us (3%)
    pallas_call x1, Pallas kernels, per_device(): pl.pallas_call(kernel, out_shape=jax.ShapeDtypeStruct((32, ROWS, 256), jn...  64.9 us
    unnamed x1, local copies, waits for them, and re-layouts  1.87 us

profile of v2, /device:TPU:1, one launch (start us, length us, event | category | flops | bytes accessed | tf_op | source)
XLA Modules:
  0.0 66.7 jit_solution(5362944587209438007)
XLA Ops:
  0.0 64.9 %shard_map.46 = f32[32,16,256]{2,1,0:T(8,128)} custom-call(bf16[6,256,256]{2,1,0:T(8,128)(2,1)} %bitcast.1, bf16[32,256,256]{2,1,0:T(8,128)(2,1)} %amps.1, s32[32]{0:T(128)} %domain_hbm.1, s32[16]{0:T(128)} %count_hbm.1), custom_call_target="tpu_custom_call" | custom-call | flops 20000000000 | bytes 6000000 | tf_op jit(solution)/shard_map/pallas_call | solution.py:278
  64.9 1.9 %copy.6 = f32[32,16,256]{2,1,0:T(8,128)} copy(f32[32,16,256]{2,1,0:T(8,128)} %shard_map.46) | data formatting | bytes 1048576

commit v3 on v2

--- a/solution.py
+++ b/solution.py
@@ -26,18 +26,18 @@
     partner = me_a + 2 - 4 * zh
     z8 = zh * 4 + z
 
-    def steps(j):
-        dx = core + 2 * j
-        dz = (dx + y) % 4
-        return dx, dz, jnp.where(dz == 3, 7, dz)
-
-    def ahead(j):
-        dx, _, ring = steps(j)
+    def steps(j, h=0):
+        dz = 1 - j + 2 * core
+        ring = dz * (1 + 2 * h) if j else dz + 4 * core
+        return (dz + 4 - y) % 4, ring
+
+    def ahead(j, h=0):
+        dx, ring = steps(j, h)
         to = (z8 + ring) % 8
         return (to % 4) * 4 + (x + dx) % 4, (y * 2 + to // 4) * 2 + core
 
-    def behind(j):
-        dx, _, ring = steps(j)
+    def behind(j, h=0):
+        dx, ring = steps(j, h)
         to = (z8 + 8 - ring) % 8
         return (to % 4) * 4 + (x + 4 - dx) % 4, (y * 2 + to // 4) * 2 + core
 
@@ -61,6 +61,28 @@
         @pl.when(src[0] != me_o)
         def _():
             pl.semaphore_signal(barrier, inc=1, device_id=src, device_id_type=MESH)
+
+    @pl.when(core == 1)
+    def _():
+        pl.semaphore_signal(barrier, inc=1, device_id=behind(1, 1), device_id_type=MESH)
+
+    at_home = jnp.where(jnp.logical_and(y == 0, core == 0), 1, 0)
+    pl.semaphore_wait(barrier, 6 + core - at_home)
+
+    def fcopy(src, dst, size, n, peer):
+        return pltpu.make_async_remote_copy(
+            src_ref=fbuf.at[pl.ds(src, size)], dst_ref=fbuf.at[pl.ds(dst, size)],
+            send_sem=fsend, recv_sem=frecv.at[n], device_id=(me_o, peer), device_id_type=MESH,
+        )
+
+    def arrived(first, size, n):
+        ref = fbuf.at[pl.ds(first, size)]
+        pltpu.make_async_copy(ref, ref, frecv.at[n]).wait()
+
+    get_factor.wait()
+    fcopy(0, 12, 3, 0, up).start()
+    fcopy(3, 15, 3, 0, down).start()
+    fcopy(0, 6, 6, 1, sibling).start()
 
     def find(p, carry):
         own = domain[p]
@@ -76,50 +98,36 @@
     zero = jnp.int32(0)
     start = (zero, (zero, zero, zero))
     found = lax.fori_loop(0, 32, find, (start, start))
-
-    at_home = jnp.where(jnp.logical_and(y == 0, core == 0), 1, 0)
-    pl.semaphore_wait(barrier, 6 - at_home)
-
-    def fcopy(src, dst, size, n, peer):
-        return pltpu.make_async_remote_copy(
-            src_ref=fbuf.at[pl.ds(src, size)], dst_ref=fbuf.at[pl.ds(dst, size)],
-            send_sem=fsend, recv_sem=frecv.at[n], device_id=(me_o, peer), device_id_type=MESH,
-        )
-
-    def arrived(first, size, n):
-        ref = fbuf.at[pl.ds(first, size)]
-        pltpu.make_async_copy(ref, ref, frecv.at[n]).wait()
-
-    get_factor.wait()
-    fcopy(0, 12, 3, 0, up).start()
-    fcopy(3, 15, 3, 0, down).start()
-    fcopy(0, 6, 6, 1, sibling).start()
     get_amps.wait()
 
-    def amps_go(k):
-        for j in range(2):
-            src, dst = packed.at[j, k], arecv.at[2 * k + j]
+    for j in range(2):
+        for k in range(CAP):
             packed[j, k] = ampv[found[j][1][k]]
 
-            @pl.when(targets[j][0] != me_o)
-            def _():
-                pltpu.make_async_remote_copy(
-                    src_ref=src, dst_ref=dst, send_sem=asend.at[j], recv_sem=arecv_sem.at[k],
-                    device_id=targets[j], device_id_type=MESH,
-                ).start()
-
-            @pl.when(targets[j][0] == me_o)
-            def _():
-                pltpu.make_async_copy(src, dst, arecv_sem.at[k]).start()
-
-    def amps_arrive(k):
-        ref = arecv.at[pl.ds(2 * k, 2)]
-        pltpu.make_async_copy(ref, ref, arecv_sem.at[k]).wait()
-
-    for k in range(CAP):
-        amps_go(k)
+    def amps_go(j):
+        for k in range(CAP):
+            for h in range(2):
+                half = pl.ds(128 * h, 128)
+                src, dst = packed.at[j, k, half, :], arecv.at[j * CAP + k, half, :]
+
+                @pl.when(targets[j][0] != me_o)
+                def _():
+                    pltpu.make_async_remote_copy(
+                        src_ref=src, dst_ref=dst, send_sem=asend.at[j], recv_sem=arecv_sem.at[j],
+                        device_id=ahead(j, h), device_id_type=MESH,
+                    ).start()
+
+                @pl.when(targets[j][0] == me_o)
+                def _():
+                    pltpu.make_async_copy(src, dst, arecv_sem.at[j]).start()
+
+    amps_go(0)
     fcopy(3, 24, 3, 2, up).start()
     fcopy(0, 27, 3, 2, down).start()
+
+    def amps_arrive(j):
+        ref = arecv.at[pl.ds(j * CAP, CAP)]
+        pltpu.make_async_copy(ref, ref, arecv_sem.at[j]).wait()
 
     def tell(n, device):
         pl.semaphore_signal(ready.at[n], inc=1, device_id=device, device_id_type=MESH)
@@ -141,84 +149,83 @@
     get_count.wait()
     acc[...] = jnp.zeros(acc.shape, jnp.float32)
 
-    def compute(first, size, slots):
+    def compute(j, first, size):
         b = fbuf[pl.ds(first, size)]
         tall = b.reshape(size * 256, 256)
         wide = jnp.concatenate([b[q] for q in range(size)], axis=1)
-        for s in slots:
+        for s in range(j * CAP, (j + 1) * CAP):
             half = jnp.dot(tall, arecv[s], preferred_element_type=jnp.float32).astype(jnp.bfloat16)
             half = jnp.concatenate([half[q * 256:(q + 1) * 256] for q in range(size)], axis=1)
             acc[s] += lax.dot_general(half, wide, NT, preferred_element_type=jnp.float32)
 
-    hear(0)
-    tell(1, (me_o, partner))
-
-    def places(first, stop, k):
+    def sixes(j, first, stop):
         def body(i, carry):
-            compute(6 * i, 6, (2 * k, 2 * k + 1))
+            compute(j, 6 * i, 6)
             return carry
 
         lax.fori_loop(first, stop, body, 0)
 
-    def ranks(place):
-        def body(k, carry):
-            compute(6 * place, 6, (2 * k, 2 * k + 1))
-            return carry
-
-        lax.fori_loop(0, 2, body, 0)
+    def relay(g):
+        arrived(36 + 4 * g, 2, 3 + g)
+        fcopy(36 + 4 * g, 38 + 4 * g, 2, 8 + g, sibling).start()
 
     arrived(6, 6, 1)
     amps_arrive(0)
-    places(0, 2, 0)
-    amps_arrive(1)
-    places(0, 2, 1)
+    amps_go(1)
+    sixes(0, 0, 2)
     arrived(12, 6, 0)
     for g in range(3):
         fcopy(12 + g, 36 + 4 * g, 1, 3 + g, up).start()
         fcopy(15 + g, 37 + 4 * g, 1, 3 + g, down).start()
     fcopy(12, 18, 6, 6, sibling).start()
+    hear(0)
+    tell(1, (me_o, partner))
+    sixes(0, 2, 3)
     hear(1)
     tell(2, (me_o, up))
     tell(3, (me_o, down))
-    ranks(2)
     arrived(18, 6, 6)
-    ranks(3)
-    amps_arrive(2)
+    sixes(0, 3, 4)
+    amps_arrive(1)
     hear(2)
     hear(3)
     tell(4, (me_o, up))
-    places(0, 4, 2)
+    sixes(1, 0, 2)
     hear(4)
     for j in range(2):
         @pl.when(targets[j][0] != me_o)
         def _():
             tell(5 + j, targets[j])
-
-    def relay(g):
-        arrived(36 + 4 * g, 2, 3 + g)
-        fcopy(36 + 4 * g, 38 + 4 * g, 2, 8 + g, sibling).start()
 
     arrived(24, 6, 2)
     fcopy(24, 30, 6, 7, sibling).start()
-    compute(24, 6, range(SLOTS))
+    sixes(0, 4, 5)
+    arrived(30, 6, 7)
+    sixes(0, 5, 6)
     relay(0)
-    arrived(30, 6, 7)
-    compute(30, 6, range(SLOTS))
-    for g in range(2):
-        relay(g + 1)
-        arrived(38 + 4 * g, 2, 8 + g)
-        compute(36 + 4 * g, 4, range(SLOTS))
+    sixes(1, 2, 3)
+    arrived(38, 2, 8)
+    compute(0, 36, 4)
+    relay(1)
+    sixes(1, 3, 4)
+    arrived(42, 2, 9)
+    compute(0, 40, 4)
+    relay(2)
+    compute(0, 44, 2)
+    sixes(1, 4, 5)
     for j in range(2):
         @pl.when(origins[j][0] != me_o)
         def _():
             hear(5 + j)
     arrived(46, 2, 10)
+    compute(0, 46, 2)
 
     place_here = zh * 16 + me_o
     for j in range(2):
-        compute(44, 4, range(j, SLOTS, 2))
+        if j == 1:
+            sixes(1, 5, 8)
         for k in range(CAP):
-            ebuf[j, k] = acc[2 * k + j].astype(jnp.bfloat16)
+            ebuf[j, k] = acc[j * CAP + k].astype(jnp.bfloat16)
         home = origins[j][0] == me_o
 
         def give(i, carry):
@@ -294,7 +301,7 @@
             pltpu.SemaphoreType.DMA,
             pltpu.SemaphoreType.DMA((11,)),
             pltpu.SemaphoreType.DMA((2,)),
-            pltpu.SemaphoreType.DMA((CAP,)),
+            pltpu.SemaphoreType.DMA((2,)),
             pltpu.SemaphoreType.DMA((2,)),
             pltpu.SemaphoreType.DMA,
             pltpu.SemaphoreType.DMA((4,)),

time: 66.9 us -> 65.2 us (0.975)
  Pallas kernels: 64.9 us -> 63.2 us
    pallas_call x1, Pallas kernels: 64.9 us -> 63.2 us  [per_device(): pl.pallas_call(kernel, out_shape=jax.ShapeDtypeStruct((32, ROWS, 256), jn...]
where the time goes in v3:
time: 65.2 us; the launch traced here: 65.1 us
  Pallas kernels  63.2 us (97%)
  local copies, waits for them, and re-layouts  1.87 us (3%)
    pallas_call x1, Pallas kernels, per_device(): pl.pallas_call(kernel, out_shape=jax.ShapeDtypeStruct((32, ROWS, 256), jn...  63.2 us
    unnamed x1, local copies, waits for them, and re-layouts  1.87 us

profile of v3, /device:TPU:1, one launch (start us, length us, event | category | flops | bytes accessed | tf_op | source)
XLA Modules:
  0.0 65.1 jit_solution(9433217171980939031)
XLA Ops:
  0.0 63.2 %shard_map.46 = f32[32,16,256]{2,1,0:T(8,128)} custom-call(bf16[6,256,256]{2,1,0:T(8,128)(2,1)} %bitcast.1, bf16[32,256,256]{2,1,0:T(8,128)(2,1)} %amps.1, s32[32]{0:T(128)} %domain_hbm.1, s32[16]{0:T(128)} %count_hbm.1), custom_call_target="tpu_custom_call" | custom-call | flops 20000000000 | bytes 6000000 | tf_op jit(solution)/shard_map/pallas_call | solution.py:285
  63.2 1.9 %copy.6 = f32[32,16,256]{2,1,0:T(8,128)} copy(f32[32,16,256]{2,1,0:T(8,128)} %shard_map.46) | data formatting | bytes 1048576

commit v4 on v3

--- a/solution.py
+++ b/solution.py
@@ -100,7 +100,7 @@
     found = lax.fori_loop(0, 32, find, (start, start))
     get_amps.wait()
 
-    for j in range(2):
+    def pack(j):
         for k in range(CAP):
             packed[j, k] = ampv[found[j][1][k]]
 
@@ -121,7 +121,9 @@
                 def _():
                     pltpu.make_async_copy(src, dst, arecv_sem.at[j]).start()
 
+    pack(0)
     amps_go(0)
+    pack(1)
     fcopy(3, 24, 3, 2, up).start()
     fcopy(0, 27, 3, 2, down).start()
 
@@ -147,7 +149,12 @@
 
     lax.fori_loop(0, 32, place, 0)
     get_count.wait()
+    hear(0)
+    tell(1, (me_o, partner))
     acc[...] = jnp.zeros(acc.shape, jnp.float32)
+    hear(1)
+    tell(2, (me_o, up))
+    tell(3, (me_o, down))
 
     def compute(j, first, size):
         b = fbuf[pl.ds(first, size)]
@@ -178,25 +185,20 @@
         fcopy(12 + g, 36 + 4 * g, 1, 3 + g, up).start()
         fcopy(15 + g, 37 + 4 * g, 1, 3 + g, down).start()
     fcopy(12, 18, 6, 6, sibling).start()
-    hear(0)
-    tell(1, (me_o, partner))
-    sixes(0, 2, 3)
-    hear(1)
-    tell(2, (me_o, up))
-    tell(3, (me_o, down))
-    arrived(18, 6, 6)
-    sixes(0, 3, 4)
-    amps_arrive(1)
     hear(2)
     hear(3)
     tell(4, (me_o, up))
+    sixes(0, 2, 3)
+    arrived(18, 6, 6)
+    sixes(0, 3, 4)
+    hear(4)
+    for j in range(2):
+        @pl.when(targets[j][0] != me_o)
+        def _():
+            tell(5 + j, targets[j])
+
+    amps_arrive(1)
     sixes(1, 0, 2)
-    hear(4)
-    for j in range(2):
-        @pl.when(targets[j][0] != me_o)
-        def _():
-            tell(5 + j, targets[j])
-
     arrived(24, 6, 2)
     fcopy(24, 30, 6, 7, sibling).start()
     sixes(0, 4, 5)
@@ -207,7 +209,6 @@
     arrived(38, 2, 8)
     compute(0, 36, 4)
     relay(1)
-    sixes(1, 3, 4)
     arrived(42, 2, 9)
     compute(0, 40, 4)
     relay(2)
@@ -223,6 +224,7 @@
     place_here = zh * 16 + me_o
     for j in range(2):
         if j == 1:
+            sixes(1, 3, 4)
             sixes(1, 5, 8)
         for k in range(CAP):
             ebuf[j, k] = acc[j * CAP + k].astype(jnp.bfloat16)

time: 65.2 us -> 63.6 us (0.975)
  Pallas kernels: 63.2 us -> 61.6 us
    pallas_call x1, Pallas kernels: 63.2 us -> 61.6 us  [per_device(): pl.pallas_call(kernel, out_shape=jax.ShapeDtypeStruct((32, ROWS, 256), jn...]
where the time goes in v4:
time: 63.6 us; the launch traced here: 63.5 us
  Pallas kernels  61.6 us (97%)
  local copies, waits for them, and re-layouts  1.87 us (3%)
    pallas_call x1, Pallas kernels, per_device(): pl.pallas_call(kernel, out_shape=jax.ShapeDtypeStruct((32, ROWS, 256), jn...  61.6 us
    unnamed x1, local copies, waits for them, and re-layouts  1.87 us

profile of v4, /device:TPU:1, one launch (start us, length us, event | category | flops | bytes accessed | tf_op | source)
XLA Modules:
  0.0 63.5 jit_solution(522052871662827021)
XLA Ops:
  0.0 61.6 %shard_map.46 = f32[32,16,256]{2,1,0:T(8,128)} custom-call(bf16[6,256,256]{2,1,0:T(8,128)(2,1)} %bitcast.1, bf16[32,256,256]{2,1,0:T(8,128)(2,1)} %amps.1, s32[32]{0:T(128)} %domain_hbm.1, s32[16]{0:T(128)} %count_hbm.1), custom_call_target="tpu_custom_call" | custom-call | flops 20000000000 | bytes 6000000 | tf_op jit(solution)/shard_map/pallas_call | solution.py:287
  61.6 1.9 %copy.6 = f32[32,16,256]{2,1,0:T(8,128)} copy(f32[32,16,256]{2,1,0:T(8,128)} %shard_map.46) | data formatting | bytes 1048576

commit v5 on v4

--- a/solution.py
+++ b/solution.py
@@ -205,7 +205,6 @@
     arrived(30, 6, 7)
     sixes(0, 5, 6)
     relay(0)
-    sixes(1, 2, 3)
     arrived(38, 2, 8)
     compute(0, 36, 4)
     relay(1)
@@ -224,7 +223,7 @@
     place_here = zh * 16 + me_o
     for j in range(2):
         if j == 1:
-            sixes(1, 3, 4)
+            sixes(1, 2, 4)
             sixes(1, 5, 8)
         for k in range(CAP):
             ebuf[j, k] = acc[j * CAP + k].astype(jnp.bfloat16)

time: 63.6 us -> 64.2 us (level)
  no operation moved by 1% of the time
where the time goes in v5:
time: 64.2 us; the launch traced here: 64 us
  Pallas kernels  62.2 us (97%)
  local copies, waits for them, and re-layouts  1.87 us (3%)
    pallas_call x1, Pallas kernels, per_device(): pl.pallas_call(kernel, out_shape=jax.ShapeDtypeStruct((32, ROWS, 256), jn...  62.2 us
    unnamed x1, local copies, waits for them, and re-layouts  1.87 us

profile of v5, /device:TPU:1, one launch (start us, length us, event | category | flops | bytes accessed | tf_op | source)
XLA Modules:
  0.0 64.0 jit_solution(2937075062630356648)
XLA Ops:
  0.0 62.2 %shard_map.46 = f32[32,16,256]{2,1,0:T(8,128)} custom-call(bf16[6,256,256]{2,1,0:T(8,128)(2,1)} %bitcast.1, bf16[32,256,256]{2,1,0:T(8,128)(2,1)} %amps.1, s32[32]{0:T(128)} %domain_hbm.1, s32[16]{0:T(128)} %count_hbm.1), custom_call_target="tpu_custom_call" | custom-call | flops 20000000000 | bytes 6000000 | tf_op jit(solution)/shard_map/pallas_call | solution.py:286
  62.2 1.9 %copy.6 = f32[32,16,256]{2,1,0:T(8,128)} copy(f32[32,16,256]{2,1,0:T(8,128)} %shard_map.46) | data formatting | bytes 1048576

commit v6 on v4

--- a/solution.py
+++ b/solution.py
@@ -139,22 +139,9 @@
 
     tell(0, (me_o, sibling))
 
-    def place(p, carry):
-        own = domain[p]
-        before = zero
-        for q in range(31):
-            before += jnp.where(jnp.logical_and(domain[q] == own, q < p), 1, 0)
-        rank[p] = before
-        return carry
-
-    lax.fori_loop(0, 32, place, 0)
-    get_count.wait()
     hear(0)
     tell(1, (me_o, partner))
     acc[...] = jnp.zeros(acc.shape, jnp.float32)
-    hear(1)
-    tell(2, (me_o, up))
-    tell(3, (me_o, down))
 
     def compute(j, first, size):
         b = fbuf[pl.ds(first, size)]
@@ -179,6 +166,9 @@
     arrived(6, 6, 1)
     amps_arrive(0)
     amps_go(1)
+    hear(1)
+    tell(2, (me_o, up))
+    tell(3, (me_o, down))
     sixes(0, 0, 2)
     arrived(12, 6, 0)
     for g in range(3):
@@ -250,6 +240,16 @@
 
         lax.fori_loop(0, 16, give, 0)
 
+    def place(p, carry):
+        own = domain[p]
+        before = zero
+        for q in range(31):
+            before += jnp.where(jnp.logical_and(domain[q] == own, q < p), 1, 0)
+        rank[p] = before
+        return carry
+
+    lax.fori_loop(0, 32, place, 0)
+    get_count.wait()
     def sent(ref, sem):
         pltpu.make_async_copy(ref, ref, sem).wait()
 

time: 63.6 us -> 63.6 us (level)
  no operation moved by 1% of the time
where the time goes in v6:
time: 63.6 us; the launch traced here: 63.5 us
  Pallas kernels  61.6 us (97%)
  local copies, waits for them, and re-layouts  1.87 us (3%)
    pallas_call x1, Pallas kernels, per_device(): pl.pallas_call(kernel, out_shape=jax.ShapeDtypeStruct((32, ROWS, 256), jn...  61.6 us
    unnamed x1, local copies, waits for them, and re-layouts  1.87 us

profile of v6, /device:TPU:1, one launch (start us, length us, event | category | flops | bytes accessed | tf_op | source)
XLA Modules:
  0.0 63.5 jit_solution(15595801836382564740)
XLA Ops:
  0.0 61.6 %shard_map.46 = f32[32,16,256]{2,1,0:T(8,128)} custom-call(bf16[6,256,256]{2,1,0:T(8,128)(2,1)} %bitcast.1, bf16[32,256,256]{2,1,0:T(8,128)(2,1)} %amps.1, s32[32]{0:T(128)} %domain_hbm.1, s32[16]{0:T(128)} %count_hbm.1), custom_call_target="tpu_custom_call" | custom-call | flops 20000000000 | bytes 6000000 | tf_op jit(solution)/shard_map/pallas_call | solution.py:287
  61.6 1.9 %copy.6 = f32[32,16,256]{2,1,0:T(8,128)} copy(f32[32,16,256]{2,1,0:T(8,128)} %shard_map.46) | data formatting | bytes 1048576

commit v7 on v4

--- a/solution.py
+++ b/solution.py
@@ -231,9 +231,9 @@
         home = origins[j][0] == me_o
 
         def give(i, carry):
-            a = (me_a + i) % 16
+            a = (me_a + 2 + i) % 16
             src = ebuf.at[j, :, pl.ds(pl.multiple_of(a * ROWS, ROWS), ROWS), :]
-            here = jnp.logical_and(home, i == 0)
+            here = jnp.logical_and(home, i == 14)
 
             @pl.when(jnp.logical_not(here))
             def _():

time: 63.6 us -> 64.1 us (level)
  no operation moved by 1% of the time
where the time goes in v7:
time: 64.1 us; the launch traced here: 64 us
  Pallas kernels  62.1 us (97%)
  local copies, waits for them, and re-layouts  1.87 us (3%)
    pallas_call x1, Pallas kernels, per_device(): pl.pallas_call(kernel, out_shape=jax.ShapeDtypeStruct((32, ROWS, 256), jn...  62.1 us
    unnamed x1, local copies, waits for them, and re-layouts  1.87 us

profile of v7, /device:TPU:1, one launch (start us, length us, event | category | flops | bytes accessed | tf_op | source)
XLA Modules:
  0.0 64.0 jit_solution(12685594971013627813)
XLA Ops:
  0.0 62.1 %shard_map.46 = f32[32,16,256]{2,1,0:T(8,128)} custom-call(bf16[6,256,256]{2,1,0:T(8,128)(2,1)} %bitcast.1, bf16[32,256,256]{2,1,0:T(8,128)(2,1)} %amps.1, s32[32]{0:T(128)} %domain_hbm.1, s32[16]{0:T(128)} %count_hbm.1), custom_call_target="tpu_custom_call" | custom-call | flops 20000000000 | bytes 6000000 | tf_op jit(solution)/shard_map/pallas_call | solution.py:287
  62.1 1.9 %copy.6 = f32[32,16,256]{2,1,0:T(8,128)} copy(f32[32,16,256]{2,1,0:T(8,128)} %shard_map.46) | data formatting | bytes 1048576
